TPU v7x, 32 devices: a whole 2x2x4 slice. The times are simulated.
32 devices in a mesh: energy: 4 (over x, core), atom: 8 (over z, y).
Axes of the slice: x: 2, y: 2, z: 4, core: 2. Of those that a mesh axis runs over, the one named last changes fastest.
Arguments:
- green: float32 [2, 8, 16, 128, 128], P(None, 'energy', 'atom'), may hold values from -6 to 6
- coupling: float32 [16, 6, 128, 128], P('atom'), may hold values from -0.5 to 0.5
- phonon: float32 [16, 6, 4], P('atom'), may hold values from 0.2 to 2
- neighbours: int32 [16, 6], P('atom'), may hold values from 0 to 15, as said below
Outputs:
- self_energy: float32 [2, 8, 16, 128, 128], P(None, 'energy', 'atom')
- rates: float32 [16, 128], P('atom')
Inputs may be any that keep to these rules, and one draw needn't show every extreme that they name: `neighbours`: each entry lies within 2 of its row's index and within 0 to 15; offsets +2 and -2 both occur.
All inputs are finite; a program needn't handle non-finite values.
Results may differ from a plain program's by a relative error of at most 0.000071.
Values sent between devices are 32-bit elements; how exact they have to be, the bound alone decides.
No kernel may reach another device: no remote copies, remote signals or barrier semaphores. Data moves between devices by JAX's collectives and lax.ppermute only.
A program may use at most 64 MiB of HBM per device.

v0:
```python
import jax
import jax.numpy as jnp
from jax import lax
from jax.sharding import PartitionSpec as P


def extended(shard, sides, width):
    for axis, dim in sides:
        devices, length = (lax.axis_size(axis), shard.shape[dim])
        up = [(i, (i + 1) % devices) for i in range(devices - 1)]
        down = [(j, i) for i, j in up]
        last = lax.slice_in_dim(shard, length - width, length, axis=dim)
        leading = lax.slice_in_dim(shard, 0, width, axis=dim)
        before = lax.ppermute(last, axis, up)
        after = lax.ppermute(leading, axis, down)
        shard = jnp.concatenate([before, shard, after], axis=dim)
    return shard


def per_device(green, coupling, phonon, neighbours):
    highest = lax.Precision.HIGHEST
    shifts = (-2, -1, 1, 2)
    e_local = green.shape[1]
    a_local = green.shape[2]
    section = extended(green, (("atom", 2),), 2)
    widened = extended(section, (("energy", 1),), 2)
    first_atom = lax.axis_index("atom") * a_local
    sigma = jnp.zeros_like(green)
    for slot in range(coupling.shape[1]):
        rows = neighbours[:, slot] - first_atom + 2
        near = jnp.take(widened, rows, axis=2)
        mixed = jnp.zeros_like(green)
        for step in range(4):
            start = 2 + shifts[step]
            factor = phonon[:, slot, step][None, None, :, None, None]
            mixed = mixed + factor * near[:, start : start + e_local]
        mats = coupling[:, slot]
        inner = jnp.einsum("aik,ceakl->ceail", mats, mixed, precision=highest)
        sigma = sigma + jnp.einsum("ceail,aml->ceaim", inner, mats, precision=highest)
    partial_rate = jnp.einsum("eail,eali->ai", sigma[0], green[0], precision=highest) - jnp.einsum(
        "eail,eali->ai", sigma[1], green[1], precision=highest
    )
    total_rate = lax.psum(partial_rate, "energy")
    points = e_local * lax.axis_size("energy")
    return (sigma, total_rate / (4.0 * points))


def solution(mesh):
    return jax.shard_map(
        per_device,
        mesh=mesh,
        in_specs=(
            P(None, "energy", "atom", None, None),
            P("atom", None, None, None),
            P("atom", None, None),
            P("atom", None),
        ),
        out_specs=(P(None, "energy", "atom", None, None), P("atom", None)),
        check_vma=False,
    )
```

profile of v0, /device:TPU:0, one launch (start us, length us, event | category | flops | bytes accessed | tf_op | source)
XLA Modules:
  0.0 98.0 jit_solution(7992272206021577321)
XLA Ops:
  0.6 4.9 %collective-permute-start = (f32[2,2,2,128,128]{4,3,2,1,0:T(8,128)}, f32[2,2,2,128,128]{4,3,2,1,0:T(8,128)S(1)}, u32[]{:S(2)}, u32[]{:S(2)}) collective-permute-start(f32[2,2,2,128,128]{4,3,2,1,0:T(8,128)} %param.6), channel_id=1, source_target_pairs={{0,1},{1,2},{2,3},{3,4},{4,5},{5,6},{6,7},{8,9},{9,10},{10,11},{11... | collective-permute-start | bytes 1572872 | tf_op jit(solution)/shard_map/ppermute | solution.py:14
  5.5 1.3 %collective-permute-start.1 = (f32[2,2,2,128,128]{4,3,2,1,0:T(8,128)}, f32[2,2,2,128,128]{4,3,2,1,0:T(8,128)S(1)}, u32[]{:S(2)}, u32[]{:S(2)}) collective-permute-start(f32[2,2,2,128,128]{4,3,2,1,0:T(8,128)} %param.6), channel_id=1, source_target_pairs={{1,0},{2,1},{3,2},{4,3},{5,4},{6,5},{7,6},{9,8},{10,9},{11,10},{12... | collective-permute-start | bytes 1572872 | tf_op jit(solution)/shard_map/ppermute | solution.py:15
  6.8 1.2 %add_reduce_fusion = (s32[2]{0:T(128)S(1)}, s32[2]{0:T(128)S(1)}, s32[2]{0:T(128)S(1)}, s32[2]{0:T(128)S(1)}, s32[2]{0:T(128)S(1)}, /*index=5*/s32[2]{0:T(128)S(1)}) fusion(s32[2,6]{1,0:T(2,128)} %param.9, s32[]{:T(128)S(6)} %mul.245), kind=kLoop, calls=%fused_computation.146 | loop fusion | flops 24 | bytes 100 | tf_op jit(solution)/shard_map/add | solution.py:30
  8.1 0.0 copy-start.5
  8.1 20.2 %collective-permute-done = f32[2,2,2,128,128]{4,3,2,1,0:T(8,128)S(1)} collective-permute-done((f32[2,2,2,128,128]{4,3,2,1,0:T(8,128)}, f32[2,2,2,128,128]{4,3,2,1,0:T(8,128)S(1)}, u32[]{:S(2)}, u32[]{:S(2)}) %collective-permute-start) | collective-permute-done | bytes 524320 | tf_op jit(solution)/shard_map/ppermute | solution.py:14
  28.3 1.1 %constant_dynamic-update-slice_fusion.1 = f32[2,2,6,128,128]{4,3,2,1,0:T(8,128)S(1)} fusion(f32[2,2,6,128,128]{4,3,2,1,0:T(8,128)S(1)} %constant_dynamic-update-slice_fusion.2, f32[2,2,2,128,128]{4,3,2,1,0:T(8,128)} %param.6), kind=kLoop, calls=%fused_computation.123 | loop fusion | bytes 1048576
  29.3 0.0 collective-permute-done.1
  29.4 1.3 %collective-permute-start.3 = (f32[2,2,6,128,128]{4,3,2,1,0:T(8,128)S(1)}, f32[2,2,6,128,128]{4,3,2,1,0:T(8,128)S(1)}, u32[]{:S(2)}, u32[]{:S(2)}) collective-permute-start(f32[2,2,6,128,128]{4,3,2,1,0:T(8,128)S(1)} %constant_dynamic-update-slice_fusion), channel_id=1, source_target_pairs={{8,0},{16,8},{24,16},{9,1},{17,9},{25,17},{10,2},{18,10},{26,18},{... | collective-permute-start | bytes 4718600 | tf_op jit(solution)/shard_map/ppermute | solution.py:15
  30.7 3.1 %collective-permute-start.2 = (f32[2,2,6,128,128]{4,3,2,1,0:T(8,128)S(1)}, f32[2,2,6,128,128]{4,3,2,1,0:T(8,128)S(1)}, u32[]{:S(2)}, u32[]{:S(2)}) collective-permute-start(f32[2,2,6,128,128]{4,3,2,1,0:T(8,128)S(1)} %constant_dynamic-update-slice_fusion), channel_id=1, source_target_pairs={{0,8},{8,16},{16,24},{1,9},{9,17},{17,25},{2,10},{10,18},{18,26},{... | collective-permute-start | bytes 4718600 | tf_op jit(solution)/shard_map/ppermute | solution.py:14
  33.9 0.0 copy-done.5
  33.9 0.2 slice_reduce_fusion.1
  34.1 0.2 slice_reduce_fusion.3
  34.4 0.3 collective-permute-done.3
  34.7 2.1 %collective-permute-done.2 = f32[2,2,6,128,128]{4,3,2,1,0:T(8,128)S(1)} collective-permute-done((f32[2,2,6,128,128]{4,3,2,1,0:T(8,128)S(1)}, f32[2,2,6,128,128]{4,3,2,1,0:T(8,128)S(1)}, u32[]{:S(2)}, u32[]{:S(2)}) %collective-permute-start.2) | collective-permute-done | bytes 1572896 | tf_op jit(solution)/shard_map/ppermute | solution.py:14
  36.8 2.4 %pad_maximum_fusion = f32[2,6,6,128,128]{4,3,2,1,0:T(8,128)} fusion(f32[2,2,6,128,128]{4,3,2,1,0:T(8,128)S(1)} %collective-permute-done.3, f32[2,2,6,128,128]{4,3,2,1,0:T(8,128)S(1)} %constant_dynamic-update-slice_fusion, f32[2,2,6,128,128]{4,3,2,1,0:T(8,128)S(1)} %collective-permute-done.2), kind=kLoop, calls=%fused_computation.6 | loop fusion | flops 2359296 | bytes 9437184 | tf_op jit(solution)/shard_map/concatenate | solution.py:16
  39.2 3.0 %gather_fusion = f32[2,2,6,128,128]{4,3,2,1,0:T(8,128)S(1)} fusion(f32[2,6,6,128,128]{4,3,2,1,0:T(8,128)} %pad_maximum_fusion, s32[1024]{0:T(1024)S(1)} %pad_clamp_fusion.5), kind=kCustom, calls=%fused_computation.clone | custom fusion | bytes 3145736 | tf_op jit(solution)/shard_map/jit(_take)/gather | solution.py:31
  42.2 0.2 select_bitcast_fusion.5
  42.4 1.7 %convolution_bitcast_fusion.5 = f32[2,2,2,128,128]{4,3,1,0,2:T(8,128)S(1)} fusion(f32[2,6,2,128,128]{4,3,1,0,2:T(8,128)S(1)} %select_bitcast_fusion.5, f32[2]{0:T(128)S(1)} %get-tuple-element.27, f32[2]{0:T(128)S(1)} %get-tuple-element.29, f32[2]{0:T(128)S(1)} %get-tuple-element.30, f32[2]{0:T(128)S(1)} %get-tuple-element.31, f32[2,6,128,128]{3,2,1,0:T(8,128)} %param.7), kind=kOutput, calls=%fused_computation.18 | convolution fusion | flops 202244096 | bytes 2754560 | tf_op jit(solution)/shard_map/aik,ceakl->ceail/dot_general | solution.py:38
  44.1 2.3 %fusion.73 = f32[2,2,2,128,128]{4,3,2,1,0:T(8,128)} fusion(f32[2,2,2,128,128]{4,3,1,0,2:T(8,128)S(1)} %convolution_bitcast_fusion.5, f32[2,6,128,128]{3,2,1,0:T(8,128)} %param.7), kind=kOutput, calls=%fused_computation.107 | convolution fusion | flops 201326592 | bytes 1179648 | tf_op jit(solution)/shard_map/ceail,aml->ceaim/dot_general | solution.py:39
  46.4 4.2 %gather_fusion.1 = f32[2,2,6,128,128]{4,3,2,1,0:T(8,128)} fusion(f32[2,6,6,128,128]{4,3,2,1,0:T(8,128)} %pad_maximum_fusion, s32[1024]{0:T(1024)S(1)} %pad_clamp_fusion.4), kind=kCustom, calls=%fused_computation.1.clone | custom fusion | bytes 3145736 | tf_op jit(solution)/shard_map/jit(_take)/gather | solution.py:31
  50.6 4.1 %gather_fusion.2 = f32[2,2,6,128,128]{4,3,2,1,0:T(8,128)} fusion(f32[2,6,6,128,128]{4,3,2,1,0:T(8,128)} %pad_maximum_fusion, s32[1024]{0:T(1024)S(1)} %pad_clamp_fusion.3), kind=kCustom, calls=%fused_computation.2.clone | custom fusion | bytes 3145736 | tf_op jit(solution)/shard_map/jit(_take)/gather | solution.py:31
  54.7 4.2 %gather_fusion.3 = f32[2,2,6,128,128]{4,3,2,1,0:T(8,128)} fusion(f32[2,6,6,128,128]{4,3,2,1,0:T(8,128)} %pad_maximum_fusion, s32[1024]{0:T(1024)S(1)} %pad_clamp_fusion.2), kind=kCustom, calls=%fused_computation.3.clone | custom fusion | bytes 3145736 | tf_op jit(solution)/shard_map/jit(_take)/gather | solution.py:31
  58.9 3.0 %gather_fusion.4 = f32[2,2,6,128,128]{4,3,2,1,0:T(8,128)S(1)} fusion(f32[2,6,6,128,128]{4,3,2,1,0:T(8,128)} %pad_maximum_fusion, s32[1024]{0:T(1024)S(1)} %pad_clamp_fusion.1), kind=kCustom, calls=%fused_computation.4.clone | custom fusion | bytes 3145736 | tf_op jit(solution)/shard_map/jit(_take)/gather | solution.py:31
  61.9 3.0 %gather_fusion.5 = f32[2,2,6,128,128]{4,3,2,1,0:T(8,128)S(1)} fusion(f32[2,6,6,128,128]{4,3,2,1,0:T(8,128)} %pad_maximum_fusion, s32[1024]{0:T(1024)S(1)} %pad_clamp_fusion), kind=kCustom, calls=%fused_computation.5.clone | custom fusion | bytes 3145736 | tf_op jit(solution)/shard_map/jit(_take)/gather | solution.py:31
  64.9 0.0 copy-start.4
  64.9 0.0 copy-start.3
  64.9 1.7 %select_bitcast_fusion.4 = f32[2,6,2,128,128]{4,3,1,0,2:T(8,128)S(1)} fusion(f32[2,2,6,128,128]{4,3,2,1,0:T(8,128)} %gather_fusion.1, pred[2]{0:T(512)(128)(4,1)S(1)} %get-tuple-element.51), kind=kLoop, calls=%fused_computation.11 | loop fusion | flops 393216 | bytes 3145730 | tf_op jit(solution)/shard_map/jit(_take)/select_n | solution.py:31
  66.7 0.0 copy-done.4
  66.7 0.0 copy-start.1
  66.7 0.8 convolution_bitcast_fusion.4
  67.5 0.0 copy-done.3
  67.5 0.6 convolution_add_fusion.4
  68.1 0.0 copy-done.1
  68.1 0.2 select_bitcast_fusion.3
  68.4 0.0 copy-start
  68.4 0.8 convolution_bitcast_fusion.3
  69.2 0.6 convolution_add_fusion.3
  69.8 0.0 copy-done
  69.8 0.2 select_bitcast_fusion.2
  70.0 0.8 convolution_bitcast_fusion.2
  70.8 0.6 convolution_add_fusion.2
  71.4 0.2 select_bitcast_fusion.1
  71.7 0.8 convolution_bitcast_fusion.1
  72.5 0.6 convolution_add_fusion.1
  73.1 0.2 select_bitcast_fusion
  73.3 0.8 convolution_bitcast_fusion
  74.1 0.6 fusion
  74.7 0.0 copy-start.2
  74.7 0.8 copy.19
  75.6 0.1 copy.37
  75.7 0.1 copy.31
  75.9 0.1 copy-done.2
  76.0 0.1 fusion.37
  76.0 21.4 %psum.7 = f32[2,128]{1,0:T(2,128)S(1)} all-reduce(f32[2,128]{1,0:T(2,128)S(1)} %sub.42), channel_id=1, replica_groups=mesh['energy'=4,'atom'=8] {'energy'}, use_global_device_ids=true, to_apply=%region_0.0 | all-reduce | flops 256 | bytes 2048 | tf_op jit(solution)/shard_map/psum | solution.py:43
  97.4 0.6 broadcast_multiply_fusion
  (16 shorter events, 0.2 us)
Async XLA Ops:
  0.6 27.6 %collective-permute-start = (f32[2,2,2,128,128]{4,3,2,1,0:T(8,128)}, f32[2,2,2,128,128]{4,3,2,1,0:T(8,128)S(1)}, u32[]{:S(2)}, u32[]{:S(2)}) collective-permute-start(f32[2,2,2,128,128]{4,3,2,1,0:T(8,128)} %param.6), channel_id=1, source_target_pairs={{0,1},{1,2},{2,3},{3,4},{4,5},{5,6},{6,7},{8,9},{9,10},{10,11},{11... | collective-permute-start | bytes 1572872 | tf_op jit(solution)/shard_map/ppermute | solution.py:14
  5.5 23.8 %collective-permute-start.1 = (f32[2,2,2,128,128]{4,3,2,1,0:T(8,128)}, f32[2,2,2,128,128]{4,3,2,1,0:T(8,128)S(1)}, u32[]{:S(2)}, u32[]{:S(2)}) collective-permute-start(f32[2,2,2,128,128]{4,3,2,1,0:T(8,128)} %param.6), channel_id=1, source_target_pairs={{1,0},{2,1},{3,2},{4,3},{5,4},{6,5},{7,6},{9,8},{10,9},{11,10},{12... | collective-permute-start | bytes 1572872 | tf_op jit(solution)/shard_map/ppermute | solution.py:15
  8.1 25.9 %copy-start.5 = (f32[2,6,4]{1,2,0:T(4,128)S(1)}, f32[2,6,4]{1,2,0:T(4,128)}, u32[]{:S(2)}) copy-start(f32[2,6,4]{1,2,0:T(4,128)} %param.8) | copy-start | bytes 580
  29.4 5.3 %collective-permute-start.3 = (f32[2,2,6,128,128]{4,3,2,1,0:T(8,128)S(1)}, f32[2,2,6,128,128]{4,3,2,1,0:T(8,128)S(1)}, u32[]{:S(2)}, u32[]{:S(2)}) collective-permute-start(f32[2,2,6,128,128]{4,3,2,1,0:T(8,128)S(1)} %constant_dynamic-update-slice_fusion), channel_id=1, source_target_pairs={{8,0},{16,8},{24,16},{9,1},{17,9},{25,17},{10,2},{18,10},{26,18},{... | collective-permute-start | bytes 4718600 | tf_op jit(solution)/shard_map/ppermute | solution.py:15
  30.7 6.1 %collective-permute-start.2 = (f32[2,2,6,128,128]{4,3,2,1,0:T(8,128)S(1)}, f32[2,2,6,128,128]{4,3,2,1,0:T(8,128)S(1)}, u32[]{:S(2)}, u32[]{:S(2)}) collective-permute-start(f32[2,2,6,128,128]{4,3,2,1,0:T(8,128)S(1)} %constant_dynamic-update-slice_fusion), channel_id=1, source_target_pairs={{0,8},{8,16},{16,24},{1,9},{9,17},{17,25},{2,10},{10,18},{18,26},{... | collective-permute-start | bytes 4718600 | tf_op jit(solution)/shard_map/ppermute | solution.py:14
  64.9 1.8 %copy-start.4 = (f32[2,6,128,128]{3,2,1,0:T(8,128)S(1)}, f32[2,6,128,128]{3,2,1,0:T(8,128)}, u32[]{:S(2)}) copy-start(f32[2,6,128,128]{3,2,1,0:T(8,128)} %param.7) | copy-start | bytes 2359300
  64.9 2.6 %copy-start.3 = (f32[2,2,2,128,128]{4,3,2,1,0:T(8,128)S(1)}, f32[2,2,2,128,128]{4,3,2,1,0:T(8,128)}, u32[]{:S(2)}) copy-start(f32[2,2,2,128,128]{4,3,2,1,0:T(8,128)} %fusion.73) | copy-start | bytes 1572868
  66.7 1.4 %copy-start.1 = (f32[2,2,6,128,128]{4,3,2,1,0:T(8,128)S(1)}, f32[2,2,6,128,128]{4,3,2,1,0:T(8,128)}, u32[]{:S(2)}) copy-start(f32[2,2,6,128,128]{4,3,2,1,0:T(8,128)} %gather_fusion.2) | copy-start | bytes 4718596
  68.4 1.4 %copy-start = (f32[2,2,6,128,128]{4,3,2,1,0:T(8,128)S(1)}, f32[2,2,6,128,128]{4,3,2,1,0:T(8,128)}, u32[]{:S(2)}) copy-start(f32[2,2,6,128,128]{4,3,2,1,0:T(8,128)} %gather_fusion.3) | copy-start | bytes 4718596
  74.7 1.2 %copy-start.2 = (f32[2,2,2,128,128]{4,3,2,1,0:T(8,128)S(1)}, f32[2,2,2,128,128]{4,3,2,1,0:T(8,128)}, u32[]{:S(2)}) copy-start(f32[2,2,2,128,128]{4,3,2,1,0:T(8,128)} %param.6) | copy-start | bytes 1572868
where the time goes:
time: 98.8 us; the launch traced here: 98 us
  local copies, waits for them, and re-layouts  24.2 us (24%)
  waiting for transfers between devices  22.6 us (23%)
  blocking collectives  21.4 us (22%)
  matrix products  10.9 us (11%)
  starting transfers between devices  10.6 us (11%)
  other arithmetic  7.22 us (7%)
  between operations  1.06 us (1%)
    ppermute x2, waiting for transfers between devices, extended(): before = lax.ppermute(last, axis, up)  22.2 us
    gather x6, local copies, waits for them, and re-layouts, per_device(): near = jnp.take(widened, rows, axis=2)  21.4 us
    psum x1, blocking collectives, per_device(): total_rate = lax.psum(partial_rate, 'energy')  21.4 us
    ppermute x2, starting transfers between devices, extended(): before = lax.ppermute(last, axis, up)  8.04 us
    dot_general x6, matrix products, per_device(): inner = jnp.einsum('aik,ceakl->ceail', mats, mixed, precision=highest)  5.66 us
    dot_general x6, matrix products, per_device(): jnp.einsum('ceail,aml->ceaim', inner, mats, precision=highest)  5.27 us
    select_n x9, other arithmetic, per_device(): near = jnp.take(widened, rows, axis=2)  2.93 us
    ppermute x2, starting transfers between devices, extended(): after = lax.ppermute(leading, axis, down)  2.58 us
  transfers between devices with their start and end apart: 4, of which 3 were waited for; matrix products, arithmetic and copies ran while one was open for 3% of the time, Pallas kernels for 0%

commit v1 on v0

v1 whole, which is shorter than its diff:
```python
import functools

import jax
import jax.numpy as jnp
from jax import lax
from jax.experimental import pallas as pl
from jax.experimental.pallas import tpu as pltpu
from jax.sharding import PartitionSpec as P

SHIFTS = (-2, -1, 1, 2)
REACH = max(SHIFTS)
OWN, PAIR, FAR = 0, 1, 2
VMEM = pl.BlockSpec(memory_space=pltpu.VMEM)
SMEM = pl.BlockSpec(memory_space=pltpu.SMEM)
HBM = pl.BlockSpec(memory_space=pltpu.HBM)


def halves(x):
    high = x.astype(jnp.bfloat16)
    return high, (x - high.astype(jnp.float32)).astype(jnp.bfloat16)


def swap(x, axis, first):
    low = range(first, lax.axis_size(axis) - 1, 2)
    return lax.ppermute(x, axis, [(i, i + 1) for i in low] + [(i + 1, i) for i in low])


def forward(x, axis):
    size = lax.axis_size(axis)
    ups = [(i, i + 2) for i in range(0, size - 2, 2)]
    downs = [(i + 2, i) for i in range(1, size - 2, 2)]
    return lax.ppermute(x, axis, ups + downs)


def shift(x, axis, up):
    pairs = [(i, i + 1) for i in range(lax.axis_size(axis) - 1)]
    return lax.ppermute(x, axis, pairs if up else [(j, i) for i, j in pairs])


def put_blocks(blocks, c, green):
    orb = green.shape[-1]
    for e in range(green.shape[0]):
        for a in range(green.shape[1]):
            high, low = halves(green[e, a])
            blocks[c, a, e, :, :orb] = high
            blocks[c, a, e, :, orb:] = low


def add_pairs(group, neighbours, phonon, coupling, blocks, totals, picked, size):
    atoms, slots, orb = coupling.shape[0], coupling.shape[1], coupling.shape[-1]
    e_local = blocks.shape[2]
    index = lax.axis_index("atom")
    base = index * atoms
    if group != OWN:
        upper = (index & 1) == (0 if group == PAIR else 1)
        base += jnp.where(upper, atoms, -atoms)

    def note(at, found):
        a = at // slots
        b = neighbours[a, at - a * slots] - base
        here = (b >= 0) & (b < atoms)

        @pl.when(here)
        def _():
            picked[found] = at

        return found + here.astype(jnp.int32)

    found = lax.fori_loop(0, atoms * slots, note, jnp.int32(0))

    def one(at):
        item = picked[jnp.minimum(at, found - 1)]
        live = jnp.where(at < found, 1.0, 0.0)
        a = item // slots
        j = item - a * slots
        high, low = halves(coupling[a, j])
        right = jnp.concatenate(
            [jnp.concatenate([high, high], 1), jnp.concatenate([low, low], 1)], 0
        )
        left = jnp.concatenate([high, low], 1)
        b = neighbours[a, j] - base
        for c, total in enumerate(totals):
            near = blocks[c, b].reshape(e_local * orb, 2 * orb)
            inner = lax.dot_general(
                near, right, (((1,), (1,)), ((), ())), preferred_element_type=jnp.float32
            )
            inner = inner[:, :orb] + inner[:, orb:]
            sums = [None] * (e_local + 2 * REACH)
            for e in range(e_local):
                high, low = halves(inner[e * orb : (e + 1) * orb])
                both = jnp.concatenate([high, low], 1)
                outer = jnp.dot(
                    left, jnp.concatenate([both, both], 0), preferred_element_type=jnp.float32
                )
                outer = outer[:, :orb] + outer[:, orb:]
                for k, s in enumerate(SHIFTS):
                    d = e - s + REACH
                    term = (phonon[a, k, j] * live) * outer
                    sums[d] = term if sums[d] is None else sums[d] + term
            yield total, a, sums

    def batch(step, _):
        results = [r for u in range(size) for r in one(step * size + u)]
        for total, a, sums in results:
            for d, value in enumerate(sums):
                if value is not None:
                    total[d, a] += value

    lax.fori_loop(0, (found + size - 1) // size, batch, None)


def part_kernel(green, first, second, sems):
    copies = [
        pltpu.make_async_copy(green.at[c], part, sems.at[c]) for c, part in enumerate((first, second))
    ]
    for copy in copies:
        copy.start()
    for copy in copies:
        copy.wait()


def own_kernel(neighbours, phonon, coupling, green, total0, total1, blocks, picked):
    for c, total in enumerate((total0, total1)):
        put_blocks(blocks, c, green.at[c])
        total[...] = jnp.zeros_like(total)
    add_pairs(OWN, neighbours, phonon, coupling, blocks, (total0, total1), picked, 2)


def turn(turned, c, green, below, above):
    e_local = green.shape[1]
    for a in range(green.shape[2]):
        for e in range(e_local):
            turned[REACH + e, a] = green[c, e, a].T
        for e in range(REACH):
            turned[e, a] = below[c, e, a].T
            turned[REACH + e_local + e, a] = above[c, e, a].T


def pair_kernel(neighbours, phonon, coupling, ahead0, before0, total0, blocks, picked):
    put_blocks(blocks, 0, ahead0)
    total0[...] = before0[...]
    add_pairs(PAIR, neighbours, phonon, coupling, blocks, (total0,), picked, 4)


def finish(c, total, own, core, cross):
    e_local = own.shape[1]
    odd = lax.axis_index("energy") & 1
    up = REACH + e_local
    to_core, to_cross = jnp.where(odd == 0, up, 0), jnp.where(odd == 0, 0, up)
    for e in range(REACH):
        core[c, e] = total[to_core + e]
        cross[c, e] = total[to_cross + e]
    for e in range(e_local):
        own[c, e] = total[REACH + e]


def rate_sums(total, turned, a):
    sums = total[0, a] * turned[0, a]
    for d in range(1, total.shape[0]):
        sums += total[d, a] * turned[d, a]
    return sums


def middle_kernel(
    neighbours, phonon, coupling, green, below, above, across0, ahead1, before0, before1,
    own, core, cross, partial, total1, turned1, total0, turned0, blocks, picked,
):
    turn(turned0, 0, green, below, above)
    turn(turned1, 1, green, below, above)
    total0[...] = before0[...]
    total1[...] = before1[...]
    put_blocks(blocks, 0, across0)
    add_pairs(FAR, neighbours, phonon, coupling, blocks, (total0,), picked, 4)
    put_blocks(blocks, 0, ahead1)
    add_pairs(PAIR, neighbours, phonon, coupling, blocks, (total1,), picked, 4)
    finish(0, total0, own, core, cross)
    for a in range(partial.shape[0]):
        partial[a] = rate_sums(total0, turned0, a)


def last_kernel(
    scale, neighbours, phonon, coupling, across1, turned1, partial, before1, own_in, core_in, cross_in,
    own, core, cross, rate, total1, blocks, picked,
):
    put_blocks(blocks, 0, across1)
    total1[...] = before1[...]
    add_pairs(FAR, neighbours, phonon, coupling, blocks, (total1,), picked, 4)
    finish(1, total1, own, core, cross)
    for a in range(partial.shape[0]):
        sums = partial[a] - rate_sums(total1, turned1, a)
        rate[a : a + 1, :] = jnp.sum(sums.T, axis=0, keepdims=True) * scale


def per_device(green, coupling, phonon, neighbours):
    _, e_local, a_local, orb, _ = green.shape
    points = e_local * lax.axis_size("energy")
    spread = (e_local + 2 * REACH, a_local, orb, orb)
    edge = (2, REACH, a_local, orb, orb)

    def call(kernel, out, operands, parts=1, scratch=(), aliases={}):
        return pl.pallas_call(
            kernel,
            out_shape=[jax.ShapeDtypeStruct(shape, jnp.float32) for shape in out],
            in_specs=[SMEM, SMEM] + [VMEM] * (1 + len(operands)),
            out_specs=[VMEM] * len(out),
            scratch_shapes=list(scratch)
            + [
                pltpu.VMEM((parts, a_local, e_local, orb, 2 * orb), jnp.bfloat16),
                pltpu.SMEM((a_local * neighbours.shape[1],), jnp.int32),
            ],
            input_output_aliases=aliases,
            compiler_params=pltpu.CompilerParams(vmem_limit_bytes=24 * 2**20),
            cost_estimate=pl.CostEstimate(flops=10**9, bytes_accessed=2 * 10**6, transcendentals=0),
        )(neighbours, jnp.swapaxes(phonon, 1, 2), coupling, *operands)

    green0, green1 = pl.pallas_call(
        part_kernel,
        out_shape=[jax.ShapeDtypeStruct(green.shape[1:], green.dtype)] * 2,
        in_specs=[HBM],
        out_specs=[VMEM] * 2,
        scratch_shapes=[pltpu.SemaphoreType.DMA((2,))],
        compiler_params=pltpu.CompilerParams(vmem_limit_bytes=24 * 2**20),
    )(green)
    green, green0, green1 = lax.optimization_barrier((green, green0, green1))
    below = shift(green, "energy", True)
    above = shift(green, "energy", False)
    ahead1 = swap(green1, "atom", 0)
    ahead0 = swap(green0, "atom", 0)
    ahead0, green1 = lax.optimization_barrier((ahead0, green1))
    across1 = swap(green1, "atom", 1)
    across0 = forward(ahead0, "atom")

    work = pltpu.VMEM(spread, jnp.float32)
    total0, total1 = call(own_kernel, [spread] * 2, (green,), parts=2)
    (total0,) = call(pair_kernel, [spread], (ahead0, total0), aliases={4: 0})
    own, core, cross, partial, total1, turned = call(
        middle_kernel,
        [green.shape, edge, edge, (a_local, orb, orb), spread, spread],
        (green, below, above, across0, ahead1, total0, total1),
        scratch=(work, work),
        aliases={9: 4},
    )
    own, core, cross, rate = call(
        functools.partial(last_kernel, 1.0 / (4.0 * points)),
        [green.shape, edge, edge, (a_local, orb)],
        (across1, turned, partial, total1, own, core, cross),
        scratch=(work,),
        aliases={7: 0, 8: 1, 9: 2},
    )
    from_core = swap(core, "energy", 0)
    from_cross = swap(cross, "energy", 1)
    return own + from_cross + from_core, lax.psum(rate, "energy")


def solution(mesh):
    return jax.shard_map(
        per_device,
        mesh=mesh,
        in_specs=(
            P(None, "energy", "atom", None, None),
            P("atom", None, None, None),
            P("atom", None, None),
            P("atom", None),
        ),
        out_specs=(P(None, "energy", "atom", None, None), P("atom", None)),
        check_vma=False,
    )
```

time: 98.8 us -> 43.5 us (0.44)
  the two profiles are of different devices: /device:TPU:0 before, /device:TPU:14 now
where the time goes in v1:
time: 43.5 us; the launch traced here: 43.1 us
  starting transfers between devices  14.4 us (33%)
  Pallas kernels  12.7 us (29%)
  blocking collectives  10.5 us (24%)
  waiting for transfers between devices  2.67 us (6%)
  local copies, waits for them, and re-layouts  1.14 us (3%)
  other arithmetic  0.91 us (2%)
  between operations  0.8 us (2%)
    pallas_call x4, Pallas kernels, call(): pl.pallas_call(kernel, out_shape=[jax.ShapeDtypeStruct(shape, jnp.float32...  11.6 us
    psum x1, blocking collectives, per_device(): return (own + from_cross + from_core, lax.psum(rate, 'energy'))  10.5 us
    ppermute x5, starting transfers between devices, swap(): lax.ppermute(x, axis, [(i, i + 1) for i in low] + [(i + 1, i) for i in low])  7.74 us
    ppermute x2, starting transfers between devices, shift(): return lax.ppermute(x, axis, pairs if up else [(j, i) for i, j in pairs])  4.35 us
    ppermute x5, waiting for transfers between devices, swap(): lax.ppermute(x, axis, [(i, i + 1) for i in low] + [(i + 1, i) for i in low])  2.67 us
    ppermute x1, starting transfers between devices, forward(): return lax.ppermute(x, axis, ups + downs)  2.35 us
    unnamed x8, local copies, waits for them, and re-layouts  1.14 us
    pallas_call x1, Pallas kernels, per_device(): pl.pallas_call(part_kernel, out_shape=[jax.ShapeDtypeStruct(green.shape[1...  1.05 us
  transfers between devices with their start and end apart: 8, of which 1 were waited for; matrix products, arithmetic and copies ran while one was open for 0% of the time, Pallas kernels for 23%

profile of v1, /device:TPU:14, one launch (start us, length us, event | category | flops | bytes accessed | tf_op | source)
XLA Modules:
  0.0 43.1 jit_solution(3319561877059463858)
XLA Ops:
  0.6 1.1 %shard_map.59 = (f32[2,2,128,128]{3,2,1,0:T(8,128)S(1)}, f32[2,2,128,128]{3,2,1,0:T(8,128)S(1)}) custom-call(f32[2,2,2,128,128]{4,3,2,1,0:T(8,128)} %green.3), custom_call_target="tpu_custom_call" | custom-call | tf_op jit(solution)/shard_map/pallas_call | solution.py:216
  1.7 0.0 copy-start.2
  1.7 0.0 copy-start.3
  1.7 0.6 %collective-permute-start = (f32[2,2,128,128]{3,2,1,0:T(8,128)S(1)}, f32[2,2,128,128]{3,2,1,0:T(8,128)S(1)}, u32[]{:S(2)}, u32[]{:S(2)}) collective-permute-start(f32[2,2,128,128]{3,2,1,0:T(8,128)S(1)} %get-tuple-element.23), channel_id=1, source_target_pairs={{0,1},{2,3},{4,5},{6,7},{1,0},{3,2},{5,4},{7,6},{8,9},{10,11},{12,... | collective-permute-start | bytes 786440 | tf_op jit(solution)/shard_map/ppermute | solution.py:25
  2.3 1.9 %collective-permute-start.3 = (f32[2,2,2,128,128]{4,3,2,1,0:T(8,128)}, f32[2,2,2,128,128]{4,3,2,1,0:T(8,128)S(1)}, u32[]{:S(2)}, u32[]{:S(2)}) collective-permute-start(f32[2,2,2,128,128]{4,3,2,1,0:T(8,128)} %green.3), channel_id=1, source_target_pairs={{8,0},{16,8},{24,16},{9,1},{17,9},{25,17},{10,2},{18,10},{26,18},{... | collective-permute-start | bytes 1572872 | tf_op jit(solution)/shard_map/ppermute | solution.py:37
  4.2 2.4 %collective-permute-start.2 = (f32[2,2,2,128,128]{4,3,2,1,0:T(8,128)}, f32[2,2,2,128,128]{4,3,2,1,0:T(8,128)S(1)}, u32[]{:S(2)}, u32[]{:S(2)}) collective-permute-start(f32[2,2,2,128,128]{4,3,2,1,0:T(8,128)} %green.3), channel_id=1, source_target_pairs={{0,8},{8,16},{16,24},{1,9},{9,17},{17,25},{2,10},{10,18},{18,26},{... | collective-permute-start | bytes 1572872 | tf_op jit(solution)/shard_map/ppermute | solution.py:37
  6.6 1.6 %collective-permute-start.5 = (f32[2,2,128,128]{3,2,1,0:T(8,128)S(1)}, f32[2,2,128,128]{3,2,1,0:T(8,128)S(1)}, u32[]{:S(2)}, u32[]{:S(2)}) collective-permute-start(f32[2,2,128,128]{3,2,1,0:T(8,128)S(1)} %get-tuple-element.25), channel_id=1, source_target_pairs={{0,1},{2,3},{4,5},{6,7},{1,0},{3,2},{5,4},{7,6},{8,9},{10,11},{12,... | collective-permute-start | bytes 786440 | tf_op jit(solution)/shard_map/ppermute | solution.py:25
  8.2 2.7 %collective-permute-done.ahead0 = f32[2,2,128,128]{3,2,1,0:T(8,128)S(1)} collective-permute-done((f32[2,2,128,128]{3,2,1,0:T(8,128)S(1)}, f32[2,2,128,128]{3,2,1,0:T(8,128)S(1)}, u32[]{:S(2)}, u32[]{:S(2)}) %collective-permute-start) | collective-permute-done | bytes 262176 | tf_op jit(solution)/shard_map/ppermute | solution.py:25
  10.9 2.3 %collective-permute-start.4 = (f32[2,2,128,128]{3,2,1,0:T(8,128)S(1)}, f32[2,2,128,128]{3,2,1,0:T(8,128)S(1)}, u32[]{:S(2)}, u32[]{:S(2)}) collective-permute-start(f32[2,2,128,128]{3,2,1,0:T(8,128)S(1)} %collective-permute-done.ahead0), channel_id=1, source_target_pairs={{0,2},{2,4},{4,6},{3,1},{5,3},{7,5},{8,10},{10,12},{12,14},{11,9},... | collective-permute-start | bytes 786440 | tf_op jit(solution)/shard_map/ppermute | solution.py:32
  13.2 3.6 %collective-permute-start.1 = (f32[2,2,128,128]{3,2,1,0:T(8,128)S(1)}, f32[2,2,128,128]{3,2,1,0:T(8,128)S(1)}, u32[]{:S(2)}, u32[]{:S(2)}) collective-permute-start(f32[2,2,128,128]{3,2,1,0:T(8,128)S(1)} %get-tuple-element.25), channel_id=1, source_target_pairs={{1,2},{3,4},{5,6},{2,1},{4,3},{6,5},{9,10},{11,12},{13,14},{10,9},... | collective-permute-start | bytes 786440 | tf_op jit(solution)/shard_map/ppermute | solution.py:25
  16.8 0.0 copy-done.2
  16.9 0.0 copy-done.3
  16.9 0.0 copy-start
  16.9 1.1 %copy-done = f32[2,6,128,128]{3,2,1,0:T(8,128)S(1)} copy-done((f32[2,6,128,128]{3,2,1,0:T(8,128)S(1)}, f32[2,6,128,128]{3,2,1,0:T(8,128)}, u32[]{:S(2)}) %copy-start) | copy-done | bytes 786456
  18.0 0.0 copy-start.1
  18.0 2.9 %shard_map.60 = (f32[6,2,128,128]{3,2,1,0:T(8,128)S(1)}, f32[6,2,128,128]{3,2,1,0:T(8,128)S(1)}) custom-call(s32[2,6]{1,0:T(2,128)S(1)} %copy-done.3, f32[2,4,6]{2,1,0:T(4,128)S(1)} %bitcast.1, f32[2,6,128,128]{3,2,1,0:T(8,128)S(1)} %copy-done, f32[2,2,2,128,128]{4,3,2,1,0:T(8,128)} %green.3), custom_call_target="tpu_custom_call" | custom-call | flops 1000000000 | bytes 2000000 | tf_op jit(solution)/shard_map/pallas_call | solution.py:201
  20.9 0.0 copy-done.1
  20.9 2.4 %shard_map.61.before0 = f32[6,2,128,128]{3,2,1,0:T(8,128)S(1)} custom-call(s32[2,6]{1,0:T(2,128)S(1)} %copy-done.3, f32[2,4,6]{2,1,0:T(4,128)S(1)} %bitcast.2, f32[2,6,128,128]{3,2,1,0:T(8,128)S(1)} %copy-done.1, f32[2,2,128,128]{3,2,1,0:T(8,128)S(1)} %collective-permute-done.ahead0, ...), custom_call_target="tpu_custom_call", output_to_operand_aliasing={{}: (4, {})} | custom-call | flops 1000000000 | bytes 2000000 | tf_op jit(solution)/shard_map/pallas_call | solution.py:201
  23.3 0.0 collective-permute-done.5.ahead1
  23.4 0.0 collective-permute-done.4.across0
  23.4 0.0 collective-permute-done.3.above
  23.4 0.0 collective-permute-done.2.below
  23.4 4.4 %shard_map.62 = (f32[2,2,2,128,128]{4,3,2,1,0:T(8,128)S(1)}, f32[2,2,2,128,128]{4,3,2,1,0:T(8,128)S(1)}, f32[2,2,2,128,128]{4,3,2,1,0:T(8,128)S(1)}, f32[2,128,1...) custom-call(s32[2,6]{1,0:T(2,128)S(1)} %copy-done.3, ...), custom_call_target="tpu_custom_call", output_to_operand_aliasing={{4}: (9, {})} | custom-call | flops 1000000000 | bytes 2000000 | tf_op jit(solution)/shard_map/pallas_call | solution.py:201
  27.8 0.0 collective-permute-done.1.across1
  27.8 1.9 %shard_map.63 = (f32[2,2,2,128,128]{4,3,2,1,0:T(8,128)S(1)}, f32[2,2,2,128,128]{4,3,2,1,0:T(8,128)S(1)}, f32[2,2,2,128,128]{4,3,2,1,0:T(8,128)S(1)}, f32[2,128]{1,0:T(2,128)S(1)}) custom-call(s32[2,6]{1,0:T(2,128)S(1)} %copy-done.3, f32[2,4,6]{2,1,0:T(4,128)S(1)} %bitcast.4, ...), custom_call_target="tpu_custom_call", output_to_operand_aliasing={{0}: (7, {}), {1}: (8, {}), {2}: (9, {})} | custom-call | flops 1000000000 | bytes 2000000 | tf_op jit(solution)/shard_map/pallas_call | solution.py:201
  29.7 1.9 %collective-permute-start.6 = (f32[2,2,2,128,128]{4,3,2,1,0:T(8,128)S(1)}, f32[2,2,2,128,128]{4,3,2,1,0:T(8,128)S(1)}, u32[]{:S(2)}, u32[]{:S(2)}) collective-permute-start(f32[2,2,2,128,128]{4,3,2,1,0:T(8,128)S(1)} %get-tuple-element.37), channel_id=1, source_target_pairs={{8,16},{16,8},{9,17},{17,9},{10,18},{18,10},{11,19},{19,11},{12,20... | collective-permute-start | bytes 1572872 | tf_op jit(solution)/shard_map/ppermute | solution.py:25
  31.6 0.1 collective-permute-start.7
  31.7 10.5 %psum.7 = f32[2,128]{1,0:T(2,128)} all-reduce(f32[2,128]{1,0:T(2,128)S(1)} %get-tuple-element.39), channel_id=1, replica_groups=mesh['energy'=4,'atom'=8] {'energy'}, use_global_device_ids=true, to_apply=%region_0.0 | all-reduce | flops 256 | bytes 2048 | tf_op jit(solution)/shard_map/psum | solution.py:252
  42.2 0.0 collective-permute-done.6
  42.2 0.0 collective-permute-done.7
  42.2 0.9 %add_add_fusion = f32[2,2,2,128,128]{4,3,2,1,0:T(8,128)} fusion(f32[2,2,2,128,128]{4,3,2,1,0:T(8,128)S(1)} %collective-permute-done.7, f32[2,2,2,128,128]{4,3,2,1,0:T(8,128)S(1)} %get-tuple-element.36, f32[2,2,2,128,128]{4,3,2,1,0:T(8,128)S(1)} %collective-permute-done.6), kind=kLoop, calls=%fused_computation | loop fusion | flops 262144 | bytes 2097152 | tf_op jit(solution)/shard_map/add | solution.py:252
Async XLA Ops:
  1.7 15.2 %copy-start.2 = (f32[2,6,4]{1,2,0:T(4,128)S(1)}, f32[2,6,4]{1,2,0:T(4,128)}, u32[]{:S(2)}) copy-start(f32[2,6,4]{1,2,0:T(4,128)} %param.6) | copy-start | bytes 580
  1.7 15.2 %copy-start.3 = (s32[2,6]{1,0:T(2,128)S(1)}, s32[2,6]{1,0:T(2,128)}, u32[]{:S(2)}) copy-start(s32[2,6]{1,0:T(2,128)} %neighbours.7) | copy-start | bytes 148
  1.7 9.2 %collective-permute-start = (f32[2,2,128,128]{3,2,1,0:T(8,128)S(1)}, f32[2,2,128,128]{3,2,1,0:T(8,128)S(1)}, u32[]{:S(2)}, u32[]{:S(2)}) collective-permute-start(f32[2,2,128,128]{3,2,1,0:T(8,128)S(1)} %get-tuple-element.23), channel_id=1, source_target_pairs={{0,1},{2,3},{4,5},{6,7},{1,0},{3,2},{5,4},{7,6},{8,9},{10,11},{12,... | collective-permute-start | bytes 786440 | tf_op jit(solution)/shard_map/ppermute | solution.py:25
  2.3 21.1 %collective-permute-start.3 = (f32[2,2,2,128,128]{4,3,2,1,0:T(8,128)}, f32[2,2,2,128,128]{4,3,2,1,0:T(8,128)S(1)}, u32[]{:S(2)}, u32[]{:S(2)}) collective-permute-start(f32[2,2,2,128,128]{4,3,2,1,0:T(8,128)} %green.3), channel_id=1, source_target_pairs={{8,0},{16,8},{24,16},{9,1},{17,9},{25,17},{10,2},{18,10},{26,18},{... | collective-permute-start | bytes 1572872 | tf_op jit(solution)/shard_map/ppermute | solution.py:37
  4.2 19.2 %collective-permute-start.2 = (f32[2,2,2,128,128]{4,3,2,1,0:T(8,128)}, f32[2,2,2,128,128]{4,3,2,1,0:T(8,128)S(1)}, u32[]{:S(2)}, u32[]{:S(2)}) collective-permute-start(f32[2,2,2,128,128]{4,3,2,1,0:T(8,128)} %green.3), channel_id=1, source_target_pairs={{0,8},{8,16},{16,24},{1,9},{9,17},{17,25},{2,10},{10,18},{18,26},{... | collective-permute-start | bytes 1572872 | tf_op jit(solution)/shard_map/ppermute | solution.py:37
  6.6 16.7 %collective-permute-start.5 = (f32[2,2,128,128]{3,2,1,0:T(8,128)S(1)}, f32[2,2,128,128]{3,2,1,0:T(8,128)S(1)}, u32[]{:S(2)}, u32[]{:S(2)}) collective-permute-start(f32[2,2,128,128]{3,2,1,0:T(8,128)S(1)} %get-tuple-element.25), channel_id=1, source_target_pairs={{0,1},{2,3},{4,5},{6,7},{1,0},{3,2},{5,4},{7,6},{8,9},{10,11},{12,... | collective-permute-start | bytes 786440 | tf_op jit(solution)/shard_map/ppermute | solution.py:25
  10.9 12.5 %collective-permute-start.4 = (f32[2,2,128,128]{3,2,1,0:T(8,128)S(1)}, f32[2,2,128,128]{3,2,1,0:T(8,128)S(1)}, u32[]{:S(2)}, u32[]{:S(2)}) collective-permute-start(f32[2,2,128,128]{3,2,1,0:T(8,128)S(1)} %collective-permute-done.ahead0), channel_id=1, source_target_pairs={{0,2},{2,4},{4,6},{3,1},{5,3},{7,5},{8,10},{10,12},{12,14},{11,9},... | collective-permute-start | bytes 786440 | tf_op jit(solution)/shard_map/ppermute | solution.py:32
  13.2 14.6 %collective-permute-start.1 = (f32[2,2,128,128]{3,2,1,0:T(8,128)S(1)}, f32[2,2,128,128]{3,2,1,0:T(8,128)S(1)}, u32[]{:S(2)}, u32[]{:S(2)}) collective-permute-start(f32[2,2,128,128]{3,2,1,0:T(8,128)S(1)} %get-tuple-element.25), channel_id=1, source_target_pairs={{1,2},{3,4},{5,6},{2,1},{4,3},{6,5},{9,10},{11,12},{13,14},{10,9},... | collective-permute-start | bytes 786440 | tf_op jit(solution)/shard_map/ppermute | solution.py:25
  16.9 1.1 %copy-start = (f32[2,6,128,128]{3,2,1,0:T(8,128)S(1)}, f32[2,6,128,128]{3,2,1,0:T(8,128)}, u32[]{:S(2)}) copy-start(f32[2,6,128,128]{3,2,1,0:T(8,128)} %coupling.7) | copy-start | bytes 2359300
  18.0 2.9 %copy-start.1 = (f32[2,6,128,128]{3,2,1,0:T(8,128)S(1)}, f32[2,6,128,128]{3,2,1,0:T(8,128)}, u32[]{:S(2)}) copy-start(f32[2,6,128,128]{3,2,1,0:T(8,128)} %coupling.7) | copy-start | bytes 2359300
  29.7 12.5 %collective-permute-start.6 = (f32[2,2,2,128,128]{4,3,2,1,0:T(8,128)S(1)}, f32[2,2,2,128,128]{4,3,2,1,0:T(8,128)S(1)}, u32[]{:S(2)}, u32[]{:S(2)}) collective-permute-start(f32[2,2,2,128,128]{4,3,2,1,0:T(8,128)S(1)} %get-tuple-element.37), channel_id=1, source_target_pairs={{8,16},{16,8},{9,17},{17,9},{10,18},{18,10},{11,19},{19,11},{12,20... | collective-permute-start | bytes 1572872 | tf_op jit(solution)/shard_map/ppermute | solution.py:25
  31.6 10.6 %collective-permute-start.7 = (f32[2,2,2,128,128]{4,3,2,1,0:T(8,128)S(1)}, f32[2,2,2,128,128]{4,3,2,1,0:T(8,128)S(1)}, u32[]{:S(2)}, u32[]{:S(2)}) collective-permute-start(f32[2,2,2,128,128]{4,3,2,1,0:T(8,128)S(1)} %get-tuple-element.38), channel_id=1, source_target_pairs={{0,8},{16,24},{8,0},{24,16},{1,9},{17,25},{9,1},{25,17},{2,10},{18... | collective-permute-start | bytes 1572872 | tf_op jit(solution)/shard_map/ppermute | solution.py:25

commit v2 on v1

v2 whole, which is shorter than its diff:
```python
import functools

import jax
import jax.numpy as jnp
from jax import lax
from jax.experimental import pallas as pl
from jax.experimental.pallas import tpu as pltpu
from jax.sharding import PartitionSpec as P

SHIFTS = (-2, -1, 1, 2)
REACH = max(SHIFTS)
OWN, PAIR, FAR = 0, 1, 2
VMEM = pl.BlockSpec(memory_space=pltpu.VMEM)
SMEM = pl.BlockSpec(memory_space=pltpu.SMEM)
HBM = pl.BlockSpec(memory_space=pltpu.HBM)


def halves(x):
    high = x.astype(jnp.bfloat16)
    return high, (x - high.astype(jnp.float32)).astype(jnp.bfloat16)


def swap(x, axis, first):
    low = range(first, lax.axis_size(axis) - 1, 2)
    return lax.ppermute(x, axis, [(i, i + 1) for i in low] + [(i + 1, i) for i in low])


def forward(x, axis):
    size = lax.axis_size(axis)
    ups = [(i, i + 2) for i in range(0, size - 2, 2)]
    downs = [(i + 2, i) for i in range(1, size - 2, 2)]
    return lax.ppermute(x, axis, ups + downs)


def shift(x, axis, up):
    pairs = [(i, i + 1) for i in range(lax.axis_size(axis) - 1)]
    return lax.ppermute(x, axis, pairs if up else [(j, i) for i, j in pairs])


def put_blocks(blocks, c, green):
    orb = green.shape[-1]
    for e in range(green.shape[0]):
        for a in range(green.shape[1]):
            high, low = halves(green[e, a])
            blocks[c, a, e, :, :orb] = high
            blocks[c, a, e, :, orb:] = low


def add_pairs(group, neighbours, phonon, coupling, blocks, totals, picked, size):
    atoms, slots, orb = coupling.shape[0], coupling.shape[1], coupling.shape[-1]
    e_local = blocks.shape[2]
    index = lax.axis_index("atom")
    base = index * atoms
    if group != OWN:
        upper = (index & 1) == (0 if group == PAIR else 1)
        base += jnp.where(upper, atoms, -atoms)

    found = jnp.int32(0)
    for a in range(atoms):
        for j in range(slots):
            picked[found] = a * slots + j
            b = neighbours[a, j] - base
            found += ((b >= 0) & (b < atoms)).astype(jnp.int32)

    def batch(step, _):
        pairs = []
        for u in range(size):
            at = step * size + u
            item = picked[jnp.minimum(at, found - 1)]
            a = item // slots
            j = item - a * slots
            high, low = halves(coupling[a, j])
            left = jnp.concatenate([high, low], 1)
            right = jnp.concatenate(
                [jnp.concatenate([high, high], 1), jnp.concatenate([low, low], 1)], 0
            )
            pairs.append((a, j, neighbours[a, j] - base, jnp.where(at < found, 1.0, 0.0), left, right))
        inners = []
        for a, j, b, live, left, right in pairs:
            for c in range(len(totals)):
                near = blocks[c, b].reshape(e_local * orb, 2 * orb)
                inner = lax.dot_general(
                    near, right, (((1,), (1,)), ((), ())), preferred_element_type=jnp.float32
                )
                inners.append(inner[:, :orb] + inner[:, orb:])
        results = []
        for a, j, b, live, left, right in pairs:
            for total in totals:
                inner = inners.pop(0)
                sums = [None] * (e_local + 2 * REACH)
                for e in range(e_local):
                    high, low = halves(inner[e * orb : (e + 1) * orb])
                    both = jnp.concatenate([high, low], 1)
                    outer = jnp.dot(
                        left, jnp.concatenate([both, both], 0), preferred_element_type=jnp.float32
                    )
                    outer = outer[:, :orb] + outer[:, orb:]
                    for k, s in enumerate(SHIFTS):
                        d = e - s + REACH
                        term = (phonon[a, k, j] * live) * outer
                        sums[d] = term if sums[d] is None else sums[d] + term
                results.append((total, a, sums))
        for total, a, sums in results:
            for d, value in enumerate(sums):
                if value is not None:
                    total[d, a] += value

    lax.fori_loop(0, (found + size - 1) // size, batch, None)


def part_kernel(green, first, second, sems):
    copies = [
        pltpu.make_async_copy(green.at[c], part, sems.at[c]) for c, part in enumerate((first, second))
    ]
    for copy in copies:
        copy.start()
    for copy in copies:
        copy.wait()


def own_kernel(neighbours, phonon, coupling, green0, green1, total0, total1, blocks, picked):
    for c, (green, total) in enumerate(((green0, total0), (green1, total1))):
        put_blocks(blocks, c, green)
        total[...] = jnp.zeros_like(total)
    add_pairs(OWN, neighbours, phonon, coupling, blocks, (total0, total1), picked, 2)


def pair_kernel(
    neighbours, phonon, coupling, green0, green1, ahead0, ahead1, before0, before1, every,
    total0, total1, turned, below, above, sems, blocks, picked,
):
    e_local, a_local = green0.shape[0], green0.shape[1]
    me, devices = lax.axis_index("energy"), every.shape[0]
    lower, upper = jnp.maximum(me - 1, 0), jnp.minimum(me + 1, devices - 1)
    fetch_below = pltpu.make_async_copy(
        every.at[lower, :, pl.ds(e_local - REACH, REACH)], below, sems.at[0]
    )
    fetch_above = pltpu.make_async_copy(every.at[upper, :, pl.ds(0, REACH)], above, sems.at[1])
    fetch_below.start()
    fetch_above.start()
    total0[...] = before0[...]
    total1[...] = before1[...]
    put_blocks(blocks, 0, ahead0)
    put_blocks(blocks, 1, ahead1)
    add_pairs(PAIR, neighbours, phonon, coupling, blocks, (total0, total1), picked, 2)
    fetch_below.wait()
    fetch_above.wait()
    has_below, has_above = jnp.where(me > 0, 1.0, 0.0), jnp.where(me < devices - 1, 1.0, 0.0)
    for c, green in enumerate((green0, green1)):
        for a in range(a_local):
            for e in range(e_local):
                turned[c, REACH + e, a] = green[e, a].T
            for e in range(REACH):
                turned[c, e, a] = below[c, e, a].T * has_below
                turned[c, REACH + e_local + e, a] = above[c, e, a].T * has_above


def finish(c, total, own, core, cross):
    e_local = own.shape[1]
    odd = lax.axis_index("energy") & 1
    up = REACH + e_local
    to_core, to_cross = jnp.where(odd == 0, up, 0), jnp.where(odd == 0, 0, up)
    for e in range(REACH):
        core[c, e] = total[to_core + e]
        cross[c, e] = total[to_cross + e]
    for e in range(e_local):
        own[c, e] = total[REACH + e]


def rate_sums(total, turned, c, a):
    sums = total[0, a] * turned[c, 0, a]
    for d in range(1, total.shape[0]):
        sums += total[d, a] * turned[c, d, a]
    return sums


def far_kernel(
    neighbours, phonon, coupling, across0, turned, before0,
    own, core, cross, partial, total0, blocks, picked,
):
    total0[...] = before0[...]
    put_blocks(blocks, 0, across0)
    add_pairs(FAR, neighbours, phonon, coupling, blocks, (total0,), picked, 4)
    finish(0, total0, own, core, cross)
    for a in range(partial.shape[0]):
        partial[a] = rate_sums(total0, turned, 0, a)


def last_kernel(
    scale, neighbours, phonon, coupling, across1, turned, partial, before1, own_in, core_in, cross_in,
    own, core, cross, rate, total1, blocks, picked,
):
    put_blocks(blocks, 0, across1)
    total1[...] = before1[...]
    add_pairs(FAR, neighbours, phonon, coupling, blocks, (total1,), picked, 4)
    own[0] = own_in[0]
    core[0] = core_in[0]
    cross[0] = cross_in[0]
    finish(1, total1, own, core, cross)
    for a in range(partial.shape[0]):
        sums = partial[a] - rate_sums(total1, turned, 1, a)
        rate[a : a + 1, :] = jnp.sum(sums.T, axis=0, keepdims=True) * scale


def per_device(green, coupling, phonon, neighbours):
    _, e_local, a_local, orb, _ = green.shape
    points = e_local * lax.axis_size("energy")
    spread = (e_local + 2 * REACH, a_local, orb, orb)
    edge = (2, REACH, a_local, orb, orb)

    def call(kernel, out, operands, parts=1, scratch=(), far=0):
        return pl.pallas_call(
            kernel,
            out_shape=[jax.ShapeDtypeStruct(shape, jnp.float32) for shape in out],
            in_specs=[SMEM, SMEM] + [VMEM] * (1 + len(operands) - far) + [HBM] * far,
            out_specs=[VMEM] * len(out),
            scratch_shapes=list(scratch)
            + [
                pltpu.VMEM((parts, a_local, e_local, orb, 2 * orb), jnp.bfloat16),
                pltpu.SMEM((a_local * neighbours.shape[1] + 1,), jnp.int32),
            ],
            compiler_params=pltpu.CompilerParams(vmem_limit_bytes=24 * 2**20),
            cost_estimate=pl.CostEstimate(flops=10**9, bytes_accessed=2 * 10**6, transcendentals=0),
        )(neighbours, jnp.swapaxes(phonon, 1, 2), coupling, *operands)

    green0, green1 = pl.pallas_call(
        part_kernel,
        out_shape=[jax.ShapeDtypeStruct(green.shape[1:], green.dtype)] * 2,
        in_specs=[HBM],
        out_specs=[VMEM] * 2,
        scratch_shapes=[pltpu.SemaphoreType.DMA((2,))],
        compiler_params=pltpu.CompilerParams(vmem_limit_bytes=24 * 2**20),
    )(green)
    every = lax.all_gather(green, "energy")
    ahead1 = swap(green1, "atom", 0)
    ahead0 = swap(green0, "atom", 0)
    total0, total1 = call(own_kernel, [spread] * 2, (green0, green1), parts=2)
    ahead0, total0, total1 = lax.optimization_barrier((ahead0, total0, total1))
    across0 = forward(ahead0, "atom")
    across1 = forward(ahead1, "atom")

    work = pltpu.VMEM(spread, jnp.float32)
    total0, total1, turned = call(
        pair_kernel,
        [spread] * 2 + [(2,) + spread],
        (green0, green1, ahead0, ahead1, total0, total1, every),
        parts=2,
        scratch=[pltpu.VMEM(edge, jnp.float32)] * 2 + [pltpu.SemaphoreType.DMA((2,))],
        far=1,
    )
    own, core, cross, partial = call(
        far_kernel,
        [green.shape, edge, edge, (a_local, orb, orb)],
        (across0, turned, total0),
        scratch=(work,),
    )
    own, core, cross, rate = call(
        functools.partial(last_kernel, 1.0 / (4.0 * points)),
        [green.shape, edge, edge, (a_local, orb)],
        (across1, turned, partial, total1, own, core, cross),
        scratch=(work,),
    )
    from_core = swap(core, "energy", 0)
    from_cross = swap(cross, "energy", 1)
    rates = jnp.sum(lax.all_gather(rate, "energy"), axis=0)
    return own + from_cross + from_core, rates


def solution(mesh):
    return jax.shard_map(
        per_device,
        mesh=mesh,
        in_specs=(
            P(None, "energy", "atom", None, None),
            P("atom", None, None, None),
            P("atom", None, None),
            P("atom", None),
        ),
        out_specs=(P(None, "energy", "atom", None, None), P("atom", None)),
        check_vma=False,
    )
```

time: 43.5 us -> 63.7 us (1.46)
  the two profiles are of different devices: /device:TPU:14 before, /device:TPU:5 now
where the time goes in v2:
time: 63.7 us; the launch traced here: 62.5 us
  waiting for transfers between devices  16.2 us (25%)
  between operations  14.1 us (22%)
  Pallas kernels  9.64 us (15%)
  blocking collectives  9.44 us (15%)
  starting transfers between devices  6.5 us (10%)
  local copies, waits for them, and re-layouts  5.13 us (8%)
  other arithmetic  1.45 us (2%)
    all_gather x1, waiting for transfers between devices, per_device(): every = lax.all_gather(green, 'energy')  10.5 us
    pallas_call x4, Pallas kernels, call(): pl.pallas_call(kernel, out_shape=[jax.ShapeDtypeStruct(shape, jnp.float32...  9.59 us
    all_gather x1, blocking collectives, per_device(): rates = jnp.sum(lax.all_gather(rate, 'energy'), axis=0)  9.44 us
    unnamed x16, local copies, waits for them, and re-layouts  5.13 us
    ppermute x4, waiting for transfers between devices, swap(): lax.ppermute(x, axis, [(i, i + 1) for i in low] + [(i + 1, i) for i in low])  5.02 us
    ppermute x4, starting transfers between devices, swap(): lax.ppermute(x, axis, [(i, i + 1) for i in low] + [(i + 1, i) for i in low])  3.9 us
    ppermute x2, starting transfers between devices, forward(): return lax.ppermute(x, axis, ups + downs)  2.56 us
  transfers between devices with their start and end apart: 7, of which 3 were waited for; matrix products, arithmetic and copies ran while one was open for 1% of the time, Pallas kernels for 13%

profile of v2, /device:TPU:5, one launch (start us, length us, event | category | flops | bytes accessed | tf_op | source)
XLA Modules:
  0.0 62.5 jit_solution(12037717023263850833)
XLA Ops:
  7.2 0.0 all-gather.5.cloned.1.call-start
  7.2 0.0 copy-start.1
  7.2 0.7 %all-gather.5.cloned.1.call-update = ((f32[2,2,2,128,128]{4,3,2,1,0:T(8,128)}), f32[8,2,2,128,128]{4,3,2,1,0:T(8,128)}) async-update(((), (), s32[]{:S(2)}) %all-gather.5.cloned.1.call-start, f32[2,2,2,128,128]{4,3,2,1,0:T(8,128)} %green.1) | async-update | bytes 3145752
  7.9 0.0 copy-start.2
  7.9 1.0 %copy-done.2 = f32[2,2,2,128,128]{4,3,2,1,0:T(8,128)S(1)} copy-done((f32[2,2,2,128,128]{4,3,2,1,0:T(8,128)S(1)}, f32[2,2,2,128,128]{4,3,2,1,0:T(8,128)}, u32[]{:S(2)}) %copy-start.2) | copy-done | bytes 524312
  8.9 0.0 copy-start.5
  8.9 0.0 copy-start.7
  8.9 0.1 shard_map.59
  9.0 0.1 collective-permute-start.2
  9.1 1.5 %collective-permute-start = (f32[2,2,128,128]{3,2,1,0:T(8,128)S(1)}, f32[2,2,128,128]{3,2,1,0:T(8,128)S(1)}, u32[]{:S(2)}, u32[]{:S(2)}) collective-permute-start(f32[2,2,128,128]{3,2,1,0:T(8,128)S(1)} %get-tuple-element.20.green1), channel_id=1, source_target_pairs={{0,1},{2,3},{4,5},{6,7},{1,0},{3,2},{5,4},{7,6},{8,9},{10,11},{12,... | collective-permute-start | bytes 786440 | tf_op jit(solution)/shard_map/ppermute | solution.py:25
  10.5 0.0 copy-start
  10.5 1.1 %copy-done = f32[2,6,128,128]{3,2,1,0:T(8,128)S(1)} copy-done((f32[2,6,128,128]{3,2,1,0:T(8,128)S(1)}, f32[2,6,128,128]{3,2,1,0:T(8,128)}, u32[]{:S(2)}) %copy-start) | copy-done | bytes 786456
  11.7 0.0 copy-start.4
  11.7 0.7 %copy-done.4 = f32[2,6,4]{1,2,0:T(4,128)S(1)} copy-done((f32[2,6,4]{1,2,0:T(4,128)S(1)}, f32[2,6,4]{1,2,0:T(4,128)}, u32[]{:S(2)}) %copy-start.4) | copy-done | bytes 216
  12.4 0.0 copy-start.6
  12.4 0.7 %copy-done.6 = s32[2,6]{1,0:T(2,128)S(1)} copy-done((s32[2,6]{1,0:T(2,128)S(1)}, s32[2,6]{1,0:T(2,128)}, u32[]{:S(2)}) %copy-start.6) | copy-done | bytes 72
  13.0 2.6 %shard_map.60 = (f32[6,2,128,128]{3,2,1,0:T(8,128)S(1)}, f32[6,2,128,128]{3,2,1,0:T(8,128)S(1)}) custom-call(s32[2,6]{1,0:T(2,128)S(1)} %copy-done.6, f32[2,4,6]{2,1,0:T(4,128)S(1)} %bitcast.4, f32[2,6,128,128]{3,2,1,0:T(8,128)S(1)} %copy-done, f32[2,2,128,128]{3,2,1,0:T(8,128)S(1)} %get-tuple-element.21.green0, f32[2,2,128,128]{3,2,1,0:T(8,128)S(1)} %get-tuple-element.20.green1), custom_call_target="tpu_custom_call" | custom-call | flops 1000000000 | bytes 2000000 | tf_op jit(solution)/shard_map/pallas_call | solution.py:212
  15.7 0.7 %collective-permute-done.2.ahead0 = f32[2,2,128,128]{3,2,1,0:T(8,128)} collective-permute-done((f32[2,2,128,128]{3,2,1,0:T(8,128)S(1)}, f32[2,2,128,128]{3,2,1,0:T(8,128)}, u32[]{:S(2)}, u32[]{:S(2)}) %collective-permute-start.2) | collective-permute-done | bytes 262176 | tf_op jit(solution)/shard_map/ppermute | solution.py:25
  16.4 1.3 %collective-permute-start.3 = (f32[2,2,128,128]{3,2,1,0:T(8,128)}, f32[2,2,128,128]{3,2,1,0:T(8,128)}, u32[]{:S(2)}, u32[]{:S(2)}) collective-permute-start(f32[2,2,128,128]{3,2,1,0:T(8,128)} %collective-permute-done.2.ahead0), channel_id=1, source_target_pairs={{0,2},{2,4},{4,6},{3,1},{5,3},{7,5},{8,10},{10,12},{12,14},{11,9},... | collective-permute-start | bytes 786440 | tf_op jit(solution)/shard_map/ppermute | solution.py:32
  17.6 4.3 %collective-permute-done.ahead1 = f32[2,2,128,128]{3,2,1,0:T(8,128)S(1)} collective-permute-done((f32[2,2,128,128]{3,2,1,0:T(8,128)S(1)}, f32[2,2,128,128]{3,2,1,0:T(8,128)S(1)}, u32[]{:S(2)}, u32[]{:S(2)}) %collective-permute-start) | collective-permute-done | bytes 262176 | tf_op jit(solution)/shard_map/ppermute | solution.py:25
  22.0 1.3 %collective-permute-start.1 = (f32[2,2,128,128]{3,2,1,0:T(8,128)S(1)}, f32[2,2,128,128]{3,2,1,0:T(8,128)S(1)}, u32[]{:S(2)}, u32[]{:S(2)}) collective-permute-start(f32[2,2,128,128]{3,2,1,0:T(8,128)S(1)} %collective-permute-done.ahead1), channel_id=1, source_target_pairs={{0,2},{2,4},{4,6},{3,1},{5,3},{7,5},{8,10},{10,12},{12,14},{11,9},... | collective-permute-start | bytes 786440 | tf_op jit(solution)/shard_map/ppermute | solution.py:32
  23.3 10.5 %all-gather.5.cloned.1.call-done = f32[8,2,2,128,128]{4,3,2,1,0:T(8,128)} async-done(((f32[2,2,2,128,128]{4,3,2,1,0:T(8,128)}), f32[8,2,2,128,128]{4,3,2,1,0:T(8,128)}) %all-gather.5.cloned.1.call-update) | async-done | bytes 2097168 | tf_op jit(solution)/shard_map/all_gather | solution.py:234
  33.8 0.0 copy-done.1
  33.8 0.0 copy-done.5
  33.8 0.0 copy-done.7
  33.8 0.0 copy-start.3
  33.8 1.6 %copy-done.3 = f32[8,2,2,128,128]{4,3,2,1,0:T(8,128)S(1)} copy-done((f32[8,2,2,128,128]{4,3,2,1,0:T(8,128)S(1)}, f32[8,2,2,128,128]{4,3,2,1,0:T(8,128)}, u32[]{:S(2)}) %copy-start.3) | copy-done | bytes 2097176
  35.4 3.6 %shard_map.61 = (f32[6,2,128,128]{3,2,1,0:T(8,128)S(1)}, f32[6,2,128,128]{3,2,1,0:T(8,128)S(1)}, f32[2,6,2,128,128]{4,3,2,1,0:T(8,128)S(1)}) custom-call(s32[2,6]{1,0:T(2,128)S(1)} %copy-done.7, f32[2,4,6]{2,1,0:T(4,128)S(1)} %bitcast.5, f32[2,6,128,128]{3,2,1,0:T(8,128)S(1)} %copy-done.1, f32[2,2,128,128]{3,2,1,0:T(8,128)S(1)} %get-tuple-element.21.green0, ...), custom_call_target="tpu_custom_call" | custom-call | flops 1000000000 | bytes 2000000 | tf_op jit(solution)/shard_map/pallas_call | solution.py:212
  39.0 0.0 collective-permute-done.3.across0
  39.0 1.8 %shard_map.62 = (f32[2,2,2,128,128]{4,3,2,1,0:T(8,128)S(1)}, f32[2,2,2,128,128]{4,3,2,1,0:T(8,128)S(1)}, f32[2,2,2,128,128]{4,3,2,1,0:T(8,128)S(1)}, f32[2,128,128]{2,1,0:T(8,128)S(1)}) custom-call(s32[2,6]{1,0:T(2,128)S(1)} %copy-done.7, f32[2,4,6]{2,1,0:T(4,128)S(1)} %bitcast.6, f32[2,6,128,128]{3,2,1,0:T(8,128)S(1)} %copy-done.1, ...), custom_call_target="tpu_custom_call" | custom-call | flops 1000000000 | bytes 2000000 | tf_op jit(solution)/shard_map/pallas_call | solution.py:212
  40.8 0.0 collective-permute-done.1.across1
  40.8 1.5 %shard_map.63 = (f32[2,2,2,128,128]{4,3,2,1,0:T(8,128)S(1)}, f32[2,2,2,128,128]{4,3,2,1,0:T(8,128)S(1)}, f32[2,2,2,128,128]{4,3,2,1,0:T(8,128)S(1)}, f32[2,128]{1,0:T(2,128)S(1)}) custom-call(s32[2,6]{1,0:T(2,128)S(1)} %copy-done.7, f32[2,4,6]{2,1,0:T(4,128)S(1)} %bitcast.7, f32[2,6,128,128]{3,2,1,0:T(8,128)S(1)} %copy-done.1, ...), custom_call_target="tpu_custom_call" | custom-call | flops 1000000000 | bytes 2000000 | tf_op jit(solution)/shard_map/pallas_call | solution.py:212
  42.4 2.3 %collective-permute-start.4 = (f32[2,2,2,128,128]{4,3,2,1,0:T(8,128)S(1)}, f32[2,2,2,128,128]{4,3,2,1,0:T(8,128)S(1)}, u32[]{:S(2)}, u32[]{:S(2)}) collective-permute-start(f32[2,2,2,128,128]{4,3,2,1,0:T(8,128)S(1)} %get-tuple-element.35), channel_id=1, source_target_pairs={{8,16},{16,8},{9,17},{17,9},{10,18},{18,10},{11,19},{19,11},{12,20... | collective-permute-start | bytes 1572872 | tf_op jit(solution)/shard_map/ppermute | solution.py:25
  44.7 0.1 collective-permute-start.5
  44.8 9.4 %all-gather.2 = f32[4,2,128]{2,1,0:T(2,128)S(1)} all-gather(f32[1,2,128]{2,1,0:T(2,128)S(1)} %bitcast.8), channel_id=3, replica_groups=mesh['energy'=4,'atom'=8] {'energy'}, dimensions={0}, use_global_device_ids=true | all-gather | bytes 5120 | tf_op jit(solution)/shard_map/all_gather | solution.py:265
  54.2 0.6 reduce_sum.9
  54.8 0.0 collective-permute-done.4
  54.8 0.0 collective-permute-done.5
  54.8 0.9 %add_add_fusion = f32[2,2,2,128,128]{4,3,2,1,0:T(8,128)} fusion(f32[2,2,2,128,128]{4,3,2,1,0:T(8,128)S(1)} %collective-permute-done.5, f32[2,2,2,128,128]{4,3,2,1,0:T(8,128)S(1)} %get-tuple-element.34, f32[2,2,2,128,128]{4,3,2,1,0:T(8,128)S(1)} %collective-permute-done.4), kind=kLoop, calls=%fused_computation | loop fusion | flops 262144 | bytes 2097152 | tf_op jit(solution)/shard_map/add | solution.py:266
Async XLA Ops:
  7.2 26.6 %all-gather.5.cloned.1.call-start = ((), (), s32[]{:S(2)}) async-start(), calls=%async_computation | async-start | bytes 2621440 | tf_op jit(solution)/shard_map/all_gather | solution.py:234
  7.2 26.6 %copy-start.1 = (f32[2,6,128,128]{3,2,1,0:T(8,128)S(1)}, f32[2,6,128,128]{3,2,1,0:T(8,128)}, u32[]{:S(2)}) copy-start(f32[2,6,128,128]{3,2,1,0:T(8,128)} %coupling.7) | copy-start | bytes 2359300
  7.9 1.0 %copy-start.2 = (f32[2,2,2,128,128]{4,3,2,1,0:T(8,128)S(1)}, f32[2,2,2,128,128]{4,3,2,1,0:T(8,128)}, u32[]{:S(2)}) copy-start(f32[2,2,2,128,128]{4,3,2,1,0:T(8,128)} %green.1) | copy-start | bytes 1572868
  8.9 24.8 %copy-start.5 = (f32[2,6,4]{1,2,0:T(4,128)S(1)}, f32[2,6,4]{1,2,0:T(4,128)}, u32[]{:S(2)}) copy-start(f32[2,6,4]{1,2,0:T(4,128)} %param.6) | copy-start | bytes 580
  8.9 24.8 %copy-start.7 = (s32[2,6]{1,0:T(2,128)S(1)}, s32[2,6]{1,0:T(2,128)}, u32[]{:S(2)}) copy-start(s32[2,6]{1,0:T(2,128)} %neighbours.7) | copy-start | bytes 148
  9.0 7.3 %collective-permute-start.2 = (f32[2,2,128,128]{3,2,1,0:T(8,128)S(1)}, f32[2,2,128,128]{3,2,1,0:T(8,128)}, u32[]{:S(2)}, u32[]{:S(2)}) collective-permute-start(f32[2,2,128,128]{3,2,1,0:T(8,128)S(1)} %get-tuple-element.21.green0), channel_id=1, source_target_pairs={{0,1},{2,3},{4,5},{6,7},{1,0},{3,2},{5,4},{7,6},{8,9},{10,11},{12,... | collective-permute-start | bytes 786440 | tf_op jit(solution)/shard_map/ppermute | solution.py:25
  9.1 12.9 %collective-permute-start = (f32[2,2,128,128]{3,2,1,0:T(8,128)S(1)}, f32[2,2,128,128]{3,2,1,0:T(8,128)S(1)}, u32[]{:S(2)}, u32[]{:S(2)}) collective-permute-start(f32[2,2,128,128]{3,2,1,0:T(8,128)S(1)} %get-tuple-element.20.green1), channel_id=1, source_target_pairs={{0,1},{2,3},{4,5},{6,7},{1,0},{3,2},{5,4},{7,6},{8,9},{10,11},{12,... | collective-permute-start | bytes 786440 | tf_op jit(solution)/shard_map/ppermute | solution.py:25
  10.5 1.1 %copy-start = (f32[2,6,128,128]{3,2,1,0:T(8,128)S(1)}, f32[2,6,128,128]{3,2,1,0:T(8,128)}, u32[]{:S(2)}) copy-start(f32[2,6,128,128]{3,2,1,0:T(8,128)} %coupling.7) | copy-start | bytes 2359300
  11.7 0.7 %copy-start.4 = (f32[2,6,4]{1,2,0:T(4,128)S(1)}, f32[2,6,4]{1,2,0:T(4,128)}, u32[]{:S(2)}) copy-start(f32[2,6,4]{1,2,0:T(4,128)} %param.6) | copy-start | bytes 580
  12.4 0.7 %copy-start.6 = (s32[2,6]{1,0:T(2,128)S(1)}, s32[2,6]{1,0:T(2,128)}, u32[]{:S(2)}) copy-start(s32[2,6]{1,0:T(2,128)} %neighbours.7) | copy-start | bytes 148
  16.4 22.6 %collective-permute-start.3 = (f32[2,2,128,128]{3,2,1,0:T(8,128)}, f32[2,2,128,128]{3,2,1,0:T(8,128)}, u32[]{:S(2)}, u32[]{:S(2)}) collective-permute-start(f32[2,2,128,128]{3,2,1,0:T(8,128)} %collective-permute-done.2.ahead0), channel_id=1, source_target_pairs={{0,2},{2,4},{4,6},{3,1},{5,3},{7,5},{8,10},{10,12},{12,14},{11,9},... | collective-permute-start | bytes 786440 | tf_op jit(solution)/shard_map/ppermute | solution.py:32
  22.0 18.9 %collective-permute-start.1 = (f32[2,2,128,128]{3,2,1,0:T(8,128)S(1)}, f32[2,2,128,128]{3,2,1,0:T(8,128)S(1)}, u32[]{:S(2)}, u32[]{:S(2)}) collective-permute-start(f32[2,2,128,128]{3,2,1,0:T(8,128)S(1)} %collective-permute-done.ahead1), channel_id=1, source_target_pairs={{0,2},{2,4},{4,6},{3,1},{5,3},{7,5},{8,10},{10,12},{12,14},{11,9},... | collective-permute-start | bytes 786440 | tf_op jit(solution)/shard_map/ppermute | solution.py:32
  33.8 1.6 %copy-start.3 = (f32[8,2,2,128,128]{4,3,2,1,0:T(8,128)S(1)}, f32[8,2,2,128,128]{4,3,2,1,0:T(8,128)}, u32[]{:S(2)}) copy-start(f32[8,2,2,128,128]{4,3,2,1,0:T(8,128)} %all-gather.5.cloned.1.call-done) | copy-start | bytes 6291460
  42.4 12.4 %collective-permute-start.4 = (f32[2,2,2,128,128]{4,3,2,1,0:T(8,128)S(1)}, f32[2,2,2,128,128]{4,3,2,1,0:T(8,128)S(1)}, u32[]{:S(2)}, u32[]{:S(2)}) collective-permute-start(f32[2,2,2,128,128]{4,3,2,1,0:T(8,128)S(1)} %get-tuple-element.35), channel_id=1, source_target_pairs={{8,16},{16,8},{9,17},{17,9},{10,18},{18,10},{11,19},{19,11},{12,20... | collective-permute-start | bytes 1572872 | tf_op jit(solution)/shard_map/ppermute | solution.py:25
  44.7 10.1 %collective-permute-start.5 = (f32[2,2,2,128,128]{4,3,2,1,0:T(8,128)S(1)}, f32[2,2,2,128,128]{4,3,2,1,0:T(8,128)S(1)}, u32[]{:S(2)}, u32[]{:S(2)}) collective-permute-start(f32[2,2,2,128,128]{4,3,2,1,0:T(8,128)S(1)} %get-tuple-element.36), channel_id=1, source_target_pairs={{0,8},{16,24},{8,0},{24,16},{1,9},{17,25},{9,1},{25,17},{2,10},{18... | collective-permute-start | bytes 1572872 | tf_op jit(solution)/shard_map/ppermute | solution.py:25
Sparse Core Ops, SparseCore 0:
  9.6 24.1 all-gather.4
